TPU v7x, 128 devices: a whole 4x4x4 slice. The times are simulated.
128 devices in a mesh: ctx: 128 (over y, z, x, core).
Axes of the slice: x: 4, y: 4, z: 4, core: 2. Of those that a mesh axis runs over, the one named last changes fastest.
Arguments:
- context_q: bfloat16 [32768, 8192], P('ctx'), may hold values from -12 to 12
- context_k: bfloat16 [32768, 1024], P('ctx'), may hold values from -6 to 6
- context_v: bfloat16 [32768, 1024], P('ctx'), may hold values from -6 to 6
- question: bfloat16 [128, 8192], P('ctx')
- valid: int32 [128], replicated, may hold values from 1 to 256, 24576 in all
- qlen: int32 [1], replicated, may hold values from 64 to 128
Outputs:
- encoded: bfloat16 [32768, 8192], P('ctx')
- answer: bfloat16 [128, 8192], P('ctx')
All inputs are finite; a program needn't handle non-finite values.
Results may differ from a plain program's by a relative error of at most 0.006.
Values may be sent and summed in bfloat16 or wider, within the bound.
A program may use at most 128 MiB of HBM per device.

v0:
```python
import functools

import jax
import jax.numpy as jnp
from jax import lax
from jax.experimental import pallas as pl
from jax.experimental.pallas import tpu as pltpu
from jax.sharding import PartitionSpec as P

H = 64
KVH = 8
DH = 128
BLK = 256
N = 128
GROUP = H // KVH
EXP2_SCALE = 1.4426950408889634 * DH ** (-0.5)

f32 = jnp.float32
bf16 = jnp.bfloat16
MESH = pl.DeviceIdType.MESH
NT = (((1,), (1,)), ((), ()))


def stride_of(axis):
    return 2 + 6 * axis + 9 * axis * (axis - 1)


def send(src, dst, send_sem, recv_sem, device):
    pltpu.make_async_remote_copy(
        src_ref=src, dst_ref=dst, send_sem=send_sem, recv_sem=recv_sem,
        device_id=(device,), device_id_type=MESH,
    ).start()


def drain(ref, sem):
    pltpu.make_async_copy(ref, ref, sem).wait()


def comm_kernel(
    question_ref, k_ref, v_ref, valid_ref, qlen_ref,
    answer_ref, anchor_out,
    q64, kvs, kvbuf, ones, rows_in, q_all, part_out, lse_out, part_in, lse_in, fin_out, fin_in, anchor,
    s_rows, r_rows, s_q, r_q, s_kv, r_kv, s_anc, r_anc, s_part, r_part, s_lse, r_lse, s_fin, r_fin, own_sem,
):
    me = lax.axis_index("ctx")
    core = me % 2
    x = (me // 2) % 4
    z = (me // 8) % 4
    y = me // 32
    cls = (x + y + z) % 4
    head = 2 * cls + core
    line = me // 8
    member = me % 8

    barrier = pltpu.get_barrier_semaphore()

    def greet(i, carry):
        pl.semaphore_signal(barrier, inc=1, device_id=((me + 1 + i) % N,), device_id_type=MESH)
        return carry

    lax.fori_loop(0, N - 1, greet, 0)

    valid_here = valid_ref[me]
    live = lax.broadcasted_iota(jnp.int32, (BLK, DH), 0) < valid_here
    for h in range(KVH):
        cols = slice(h * DH, (h + 1) * DH)
        k_h = k_ref[:, cols].astype(f32)
        v_h = v_ref[:, cols].astype(f32)
        kvs[h * 512:h * 512 + 256, :] = jnp.where(live, k_h, k_h[0:1, :]).astype(bf16)
        kvs[h * 512 + 256:h * 512 + 512, :] = jnp.where(live, v_h, 0.0).astype(bf16)
    for h in range(H):
        q64[h:h + 1, :] = question_ref[:, h * DH:(h + 1) * DH].astype(f32)
    axis = head % 3
    stride = stride_of(axis)
    first = me - core - ((me // stride) % 4) * stride
    for b in range(8):
        valid_b = valid_ref[first + (b // 2) * stride + b % 2]
        ones[b * BLK:(b + 1) * BLK, :] = jnp.where(
            lax.broadcasted_iota(jnp.int32, (BLK, DH), 0) < valid_b, 1.0, 0.0).astype(bf16)

    pl.semaphore_wait(barrier, N - 1)

    def send_rows(d, carry):
        other = (head + d) % 8
        target = me - member + ((other // 2 + 8 - y - z) % 4) * 2 + other % 2
        send(q64.at[pl.ds(other * 8, 8)], rows_in.at[member], s_rows, r_rows, target)
        return carry

    lax.fori_loop(1, 8, send_rows, 0)
    rows_in[member] = q64[pl.ds(head * 8, 8), :]

    def send_kv(d, carry):
        other = (head + d) % 8
        step = stride_of(other % 3)
        at = (me // step) % 4
        target = me - core + ((at + other // 2 + 4 - cls) % 4 - at) * step + other % 2
        send(kvs.at[pl.ds(other * 512, 512)], kvbuf.at[pl.ds((at * 2 + core) * 512, 512)], s_kv, r_kv, target)
        return carry

    at_home = (me // stride) % 4
    own_kv = pltpu.make_async_copy(
        kvs.at[pl.ds(head * 512, 512)], kvbuf.at[pl.ds((at_home * 2 + core) * 512, 512)], own_sem)
    own_kv.start()

    @pl.when(me == 0)
    def _():
        def scatter(j, carry):
            send(kvs.at[pl.ds(32 * j, 32)], anchor.at[pl.ds(32 * j, 32)], s_anc.at[0], r_anc.at[0], 2 * j)
            return carry

        def scatter_odd(j, carry):
            piece = 2048 + 32 * (((j // 4) % 4) * 16 + (j % 4) * 4 + j // 16)
            send(kvs.at[pl.ds(piece, 32)], anchor.at[pl.ds(piece, 32)], s_anc.at[5], r_anc.at[0], 2 * j + 1)
            return carry

        lax.fori_loop(0, 64, scatter_odd, 0)
        lax.fori_loop(1, 64, scatter, 0)
        anchor[0:32, :] = kvs[0:32, :]

    lax.fori_loop(1, 8, send_kv, 0)

    drain(rows_in.at[pl.ds(0, 7)], r_rows)
    q_all[pl.ds(line * 64, 64), :] = rows_in[...].reshape(64, DH).astype(bf16)

    def peer(d):
        other = (line + d) % 16
        return other, (other * 4 + (cls + 8 - other // 4 - other % 4) % 4) * 2 + core

    def send_q(d, carry):
        other, target = peer(d)
        send(q_all.at[pl.ds(line * 64, 64)], q_all.at[pl.ds(line * 64, 64)], s_q, r_q, target)
        return carry

    lax.fori_loop(1, 16, send_q, 0)

    st = (2 + 30 * core, 8 - 6 * core, 32 - 24 * core)
    at = [(me // s) % 4 for s in st]
    half = 2048 * core
    starts = (half + 32 * (at[2] * 16 + at[1] * 4 + at[0]), half + 32 * (at[2] * 16 + at[1] * 4), half + 32 * at[2] * 16)
    sizes = (32, 128, 512)

    def gather_stage(n):
        piece = anchor.at[pl.ds(starts[n], sizes[n])]
        for d in (1, 2, 3):
            target = me + ((at[n] + d) % 4 - at[n]) * st[n]
            send(piece, piece, s_anc.at[n + 1], r_anc.at[n + 1], target)

    def gather_wait(n):
        drain(anchor.at[pl.ds(0, 3 * sizes[n])], r_anc.at[n + 1])

    @pl.when(me != 0)
    def _():
        drain(anchor.at[pl.ds(0, 32)], r_anc.at[0])

    gather_stage(0)
    gather_wait(0)
    gather_stage(1)

    drain(q_all.at[pl.ds(0, 15 * 64)], r_q)
    own_kv.wait()
    drain(kvbuf.at[pl.ds(0, 7 * 512)], r_kv)
    gather_wait(1)
    gather_stage(2)

    diag = lax.broadcasted_iota(jnp.int32, (64, DH), 0) == lax.broadcasted_iota(jnp.int32, (64, DH), 1)

    def attend(i, carry):
        rows = pl.ds(pl.multiple_of(i * 128, 128), 128)
        q = q_all[rows, :]
        s = [lax.dot_general(q, kvbuf[b * 512:b * 512 + 256, :], NT, preferred_element_type=f32) for b in range(8)]
        peak = functools.reduce(jnp.maximum, [jnp.max(s_b, axis=1, keepdims=True) for s_b in s]) * EXP2_SCALE
        p = jnp.concatenate([jnp.exp2(s_b * EXP2_SCALE - peak).astype(bf16) for s_b in s], axis=1)
        v = jnp.concatenate(
            [jnp.concatenate([kvbuf[b * 512 + 256:b * 512 + 512, :], ones[b * BLK:(b + 1) * BLK, :]], axis=1) for b in range(8)], axis=0)
        o = jnp.dot(p, v, preferred_element_type=f32)
        total = o[:, DH:]
        part_out[rows, :] = (o[:, :DH] / total).astype(bf16)
        lse = peak + jnp.log2(total)
        for n in range(2):
            flat = jnp.sum(jnp.where(diag, lse[n * 64:(n + 1) * 64], 0.0), axis=0, keepdims=True)
            lse_out[2 * i + n] = jnp.broadcast_to(flat, (8, DH))
        return carry

    lax.fori_loop(0, 8, attend, 0)

    def send_part(d, carry):
        other, target = peer(d)
        send(part_out.at[pl.ds(other * 64, 64)], part_in.at[pl.ds(line * 64, 64)], s_part, r_part, target)
        send(lse_out.at[other], lse_in.at[line], s_lse, r_lse, target)
        return carry

    lax.fori_loop(1, 16, send_part, 0)
    part_in[pl.ds(line * 64, 64), :] = part_out[pl.ds(line * 64, 64), :]
    lse_in[line] = lse_out[line]

    gather_wait(2)
    mine = anchor.at[pl.ds(half, 2048)]
    send(mine, mine, s_anc.at[4], r_anc.at[4], me + 1 - 2 * core)

    drain(part_in.at[pl.ds(0, 15 * 64)], r_part)
    drain(lse_in.at[pl.ds(0, 15)], r_lse)
    lse_all = lse_in[...]
    weight = jnp.exp2(lse_all - jnp.max(lse_all, axis=0, keepdims=True))
    weight = weight / jnp.sum(weight, axis=0, keepdims=True)
    merged = jnp.zeros((64, DH), f32)
    for j in range(16):
        column = jnp.sum(jnp.where(diag, weight[j, 0:1, :], 0.0), axis=1, keepdims=True)
        merged += column * part_in[j * 64:(j + 1) * 64, :].astype(f32)
    fin_out[...] = merged.reshape(8, 8, DH)

    def send_fin(d, carry):
        other = (member + d) % 8
        send(fin_out.at[other], fin_in.at[head], s_fin, r_fin, me - member + other)
        return carry

    lax.fori_loop(1, 8, send_fin, 0)
    fin_in[head] = fin_out[member]
    drain(fin_in.at[pl.ds(0, 7)], r_fin)
    answer_ref[...] = jnp.where(me < qlen_ref[0], fin_in[...].reshape(64, DH), 0.0)

    drain(anchor.at[pl.ds(0, 2048)], r_anc.at[4])
    anchor_out[...] = anchor[...]

    drain(rows_in.at[pl.ds(0, 7)], s_rows)
    drain(kvbuf.at[pl.ds(0, 7 * 512)], s_kv)
    drain(q_all.at[pl.ds(0, 15 * 64)], s_q)
    drain(part_in.at[pl.ds(0, 15 * 64)], s_part)
    drain(lse_in.at[pl.ds(0, 15)], s_lse)
    drain(fin_in.at[pl.ds(0, 7)], s_fin)
    for n in range(3):
        drain(anchor.at[pl.ds(0, 3 * sizes[n])], s_anc.at[n + 1])
    drain(anchor.at[pl.ds(0, 2048)], s_anc.at[4])

    @pl.when(me == 0)
    def _():
        drain(anchor.at[pl.ds(0, 63 * 32)], s_anc.at[0])
        drain(anchor.at[pl.ds(0, 2048)], s_anc.at[5])


def exchange(question, k, v, valid, qlen):
    vmem = pl.BlockSpec(memory_space=pltpu.VMEM)
    smem = pl.BlockSpec(memory_space=pltpu.SMEM)
    dma = pltpu.SemaphoreType.DMA
    return pl.pallas_call(
        comm_kernel,
        out_shape=(jax.ShapeDtypeStruct((H, DH), f32), jax.ShapeDtypeStruct((KVH * 512, DH), bf16)),
        in_specs=[vmem, vmem, vmem, smem, smem],
        out_specs=(vmem, vmem),
        scratch_shapes=[
            pltpu.VMEM((H, DH), f32),
            pltpu.VMEM((KVH * 512, DH), bf16),
            pltpu.VMEM((8 * 512, DH), bf16),
            pltpu.VMEM((8 * BLK, DH), bf16),
            pltpu.VMEM((8, 8, DH), f32),
            pltpu.VMEM((16 * 64, DH), bf16),
            pltpu.VMEM((16 * 64, DH), bf16),
            pltpu.VMEM((16, 8, DH), f32),
            pltpu.VMEM((16 * 64, DH), bf16),
            pltpu.VMEM((16, 8, DH), f32),
            pltpu.VMEM((8, 8, DH), f32),
            pltpu.VMEM((8, 8, DH), f32),
            pltpu.VMEM((KVH * 512, DH), bf16),
            dma, dma, dma, dma, dma, dma, dma((6,)), dma((5,)), dma, dma, dma, dma, dma, dma, dma,
        ],
        compiler_params=pltpu.CompilerParams(collective_id=0, has_side_effects=True, vmem_limit_bytes=40 << 20),
        name="exchange",
    )(question, k, v, valid, qlen)


def encode_kernel(valid_ref, where_ref, q_ref, k_ref, v_ref, anchor_ref, out_ref):
    position = where_ref[0]
    valid_here = valid_ref[position]
    valid_first = jnp.where(position > 0, valid_ref[0], 0)
    row = lax.broadcasted_iota(jnp.int32, (BLK, DH), 0)
    live = row < valid_here
    anchored = row < valid_first
    k_own = k_ref[...].astype(f32)
    k_own = jnp.where(live, k_own, k_own[0:1, :])
    k_first = anchor_ref[:BLK, :].astype(f32)
    k_first = jnp.where(position > 0, k_first, k_own[0:1, :])
    keys = jnp.concatenate([k_first.astype(bf16), k_own.astype(bf16)], axis=0)
    v_own = jnp.where(live, v_ref[...].astype(f32), 0.0).astype(bf16)
    v_first = jnp.where(anchored, anchor_ref[BLK:, :].astype(f32), 0.0).astype(bf16)
    values = jnp.concatenate([
        jnp.concatenate([v_first, jnp.where(anchored, 1.0, 0.0).astype(bf16)], axis=1),
        jnp.concatenate([v_own, jnp.where(live, 1.0, 0.0).astype(bf16)], axis=1),
    ], axis=0)
    causal = lax.broadcasted_iota(jnp.int32, (BLK, BLK), 1) <= lax.broadcasted_iota(jnp.int32, (BLK, BLK), 0)
    for h in range(GROUP):
        cols = slice(h * DH, (h + 1) * DH)
        s = lax.dot_general(q_ref[:, cols], keys, NT, preferred_element_type=f32)
        s_first = s[:, :BLK]
        s_own = jnp.where(causal, s[:, BLK:], -1e30)
        peak = jnp.maximum(jnp.max(s_first, axis=1, keepdims=True), jnp.max(s_own, axis=1, keepdims=True)) * EXP2_SCALE
        p = jnp.concatenate([jnp.exp2(s_first * EXP2_SCALE - peak), jnp.exp2(s_own * EXP2_SCALE - peak)], axis=1).astype(bf16)
        o = jnp.dot(p, values, preferred_element_type=f32)
        out_ref[:, cols] = jnp.where(live, o[:, :DH] / o[:, DH:], 0.0).astype(bf16)


def encode(q, k, v, anchor, valid, position):
    smem = pl.BlockSpec(memory_space=pltpu.SMEM)
    return pl.pallas_call(
        encode_kernel,
        grid=(KVH,),
        out_shape=jax.ShapeDtypeStruct((BLK, H * DH), bf16),
        in_specs=[
            smem, smem,
            pl.BlockSpec((BLK, GROUP * DH), lambda i: (0, i)),
            pl.BlockSpec((BLK, DH), lambda i: (0, i)),
            pl.BlockSpec((BLK, DH), lambda i: (0, i)),
            pl.BlockSpec((512, DH), lambda i: (i, 0)),
        ],
        out_specs=pl.BlockSpec((BLK, GROUP * DH), lambda i: (0, i)),
        compiler_params=pltpu.CompilerParams(vmem_limit_bytes=40 << 20),
        name="encode",
    )(valid, position, q, k, v, anchor)


def body(context_q, context_k, context_v, question, valid, qlen):
    answer, anchor = exchange(question, context_k, context_v, valid, qlen)
    position = lax.axis_index("ctx").reshape(1)
    encoded = encode(context_q, context_k, context_v, anchor, valid, position)
    return encoded, answer.reshape(1, H * DH).astype(bf16)


def solution(mesh):
    in_specs = (P("ctx", None), P("ctx", None), P("ctx", None), P("ctx", None), P(), P())
    out_specs = (P("ctx", None), P("ctx", None))
    return jax.shard_map(body, mesh=mesh, in_specs=in_specs, out_specs=out_specs, check_vma=False)
```

profile of v0, /device:TPU:1, one launch (start us, length us, event | category | flops | bytes accessed | tf_op | source)
XLA Modules:
  0.0 75.5 jit_solution(3069285476910401865)
XLA Ops:
  1.3 0.0 copy-start.1
  1.3 1.0 %copy-done.1 = bf16[256,1024]{1,0:T(8,128)(2,1)S(1)} copy-done((bf16[256,1024]{1,0:T(8,128)(2,1)S(1)}, bf16[256,1024]{1,0:T(8,128)(2,1)}, u32[]{:S(2)}) %copy-start.1) | copy-done | bytes 524312
  2.3 0.0 copy-start.3
  2.3 1.0 %copy-done.3 = bf16[256,1024]{1,0:T(8,128)(2,1)S(1)} copy-done((bf16[256,1024]{1,0:T(8,128)(2,1)S(1)}, bf16[256,1024]{1,0:T(8,128)(2,1)}, u32[]{:S(2)}) %copy-start.3) | copy-done | bytes 524312
  3.4 0.0 copy-start.5
  3.4 0.8 %copy-done.5 = bf16[1,8192]{1,0:T(2,128)(2,1)S(1)} copy-done((bf16[1,8192]{1,0:T(2,128)(2,1)S(1)}, bf16[1,8192]{1,0:T(2,128)(2,1)}, u32[]{:S(2)}) %copy-start.5) | copy-done | bytes 16408
  4.1 0.0 copy-start.6
  4.1 0.7 copy-done.6
  4.8 50.8 %exchange.1 = (f32[64,128]{1,0:T(8,128)S(1)}, bf16[4096,128]{1,0:T(8,128)(2,1)S(1)}) custom-call(bf16[1,8192]{1,0:T(2,128)(2,1)S(1)} %copy-done.5, bf16[256,1024]{1,0:T(8,128)(2,1)S(1)} %copy-done.1, bf16[256,1024]{1,0:T(8,128)(2,1)S(1)} %copy-done.3, s32[128]{0:T(128)S(1)} %copy-done.6, s32[1]{0:T(128)S(6)} %copy.11.qlen_ref), custom_call_target="tpu_custom_call" | custom-call | tf_op jit(solution)/shard_map/exchange/pallas_call | solution.py:244
  55.6 0.6 copy.10
  56.3 0.0 copy-start
  56.3 2.2 %copy-done = bf16[256,8192]{1,0:T(8,128)(2,1)S(1)} copy-done((bf16[256,8192]{1,0:T(8,128)(2,1)S(1)}, bf16[256,8192]{1,0:T(8,128)(2,1)}, u32[]{:S(2)}) %copy-start) | copy-done | bytes 4194328
  58.5 0.0 copy-start.2
  58.5 1.0 %copy-done.2 = bf16[256,1024]{1,0:T(8,128)(2,1)S(1)} copy-done((bf16[256,1024]{1,0:T(8,128)(2,1)S(1)}, bf16[256,1024]{1,0:T(8,128)(2,1)}, u32[]{:S(2)}) %copy-start.2) | copy-done | bytes 524312
  59.5 0.0 copy-start.4
  59.5 1.0 %copy-done.4 = bf16[256,1024]{1,0:T(8,128)(2,1)S(1)} copy-done((bf16[256,1024]{1,0:T(8,128)(2,1)S(1)}, bf16[256,1024]{1,0:T(8,128)(2,1)}, u32[]{:S(2)}) %copy-start.4) | copy-done | bytes 524312
  60.5 14.9 %encode.1 = bf16[256,8192]{1,0:T(8,128)(2,1)} custom-call(s32[128]{0:T(128)S(1)} %copy-done.6, s32[1]{0:T(128)} %bitcast.where_ref, bf16[256,8192]{1,0:T(8,128)(2,1)S(1)} %copy-done, bf16[256,1024]{1,0:T(8,128)(2,1)S(1)} %copy-done.2, bf16[256,1024]{1,0:T(8,128)(2,1)S(1)} %copy-done.4, bf16[4096,128]{1,0:T(8,128)(2,1)S(1)} %get-tuple-element.4.anchor_ref), custom_call_target="tpu_custom_call" | custom-call | tf_op jit(solution)/shard_map/encode/pallas_call | solution.py:302
  (1 shorter events, 0.0 us)
Async XLA Ops:
  1.3 1.0 %copy-start.1 = (bf16[256,1024]{1,0:T(8,128)(2,1)S(1)}, bf16[256,1024]{1,0:T(8,128)(2,1)}, u32[]{:S(2)}) copy-start(bf16[256,1024]{1,0:T(8,128)(2,1)} %k_ref.3) | copy-start | bytes 1572868
  2.3 1.0 %copy-start.3 = (bf16[256,1024]{1,0:T(8,128)(2,1)S(1)}, bf16[256,1024]{1,0:T(8,128)(2,1)}, u32[]{:S(2)}) copy-start(bf16[256,1024]{1,0:T(8,128)(2,1)} %v_ref.3) | copy-start | bytes 1572868
  3.4 0.8 %copy-start.5 = (bf16[1,8192]{1,0:T(2,128)(2,1)S(1)}, bf16[1,8192]{1,0:T(2,128)(2,1)}, u32[]{:S(2)}) copy-start(bf16[1,8192]{1,0:T(2,128)(2,1)} %question_ref.1) | copy-start | bytes 49156
  4.1 0.7 copy-start.6
  56.3 2.2 %copy-start = (bf16[256,8192]{1,0:T(8,128)(2,1)S(1)}, bf16[256,8192]{1,0:T(8,128)(2,1)}, u32[]{:S(2)}) copy-start(bf16[256,8192]{1,0:T(8,128)(2,1)} %q_ref.1) | copy-start | bytes 12582916
  58.5 1.0 %copy-start.2 = (bf16[256,1024]{1,0:T(8,128)(2,1)S(1)}, bf16[256,1024]{1,0:T(8,128)(2,1)}, u32[]{:S(2)}) copy-start(bf16[256,1024]{1,0:T(8,128)(2,1)} %k_ref.3) | copy-start | bytes 1572868
  59.5 1.0 %copy-start.4 = (bf16[256,1024]{1,0:T(8,128)(2,1)S(1)}, bf16[256,1024]{1,0:T(8,128)(2,1)}, u32[]{:S(2)}) copy-start(bf16[256,1024]{1,0:T(8,128)(2,1)} %v_ref.3) | copy-start | bytes 1572868
where the time goes:
time: 75.9 us; the launch traced here: 75.5 us
  Pallas kernels  65.8 us (87%)
  local copies, waits for them, and re-layouts  8.4 us (11%)
  between operations  1.31 us (2%)
    pallas_call x1, Pallas kernels, exchange(): pl.pallas_call(comm_kernel, out_shape=(jax.ShapeDtypeStruct((H, DH), f32)...  50.8 us
    pallas_call x1, Pallas kernels, encode(): pl.pallas_call(encode_kernel, grid=(KVH,), out_shape=jax.ShapeDtypeStruct...  14.9 us
    unnamed x15, local copies, waits for them, and re-layouts  8.4 us

commit v1 on v0

v1 whole, which is shorter than its diff:
```python
import functools

import jax
import jax.numpy as jnp
from jax import lax
from jax.experimental import pallas as pl
from jax.experimental.pallas import tpu as pltpu
from jax.sharding import PartitionSpec as P

H = 64
KVH = 8
DH = 128
BLK = 256
N = 128
GROUP = H // KVH
EXP2_SCALE = 1.4426950408889634 * DH ** (-0.5)

f32 = jnp.float32
bf16 = jnp.bfloat16
MESH = pl.DeviceIdType.MESH
NT = (((1,), (1,)), ((), ()))

ROWS_AT = 2
GATHER_1_AT = 1
GATHER_2_AT = 5
MERGE_AT = 6


def stride_of(axis):
    return 2 + 6 * axis + 9 * axis * (axis - 1)


def send(src, dst, send_sem, recv_sem, device):
    pltpu.make_async_remote_copy(
        src_ref=src, dst_ref=dst, send_sem=send_sem, recv_sem=recv_sem,
        device_id=(device,), device_id_type=MESH,
    ).start()


def drain(ref, sem):
    pltpu.make_async_copy(ref, ref, sem).wait()


def star_kernel(
    q_hbm, k_hbm, v_hbm, question_hbm, valid_hbm, qlen_ref,
    out_ref, answer_ref,
    q_ref, k_ref, v_ref, question_ref, valid_ref,
    own_out, own_lse, q64, kvs, kvbuf, ones, rows_in, q_all, part_out, lse_out, part_in, lse_in, fin_out, fin_in, anchor,
    load_sem, s_rows, r_rows, s_q, r_q, s_kv, r_kv, s_anc, r_anc, s_part, r_part, s_lse, r_lse, s_fin, r_fin, own_sem,
):
    me = lax.axis_index("ctx")
    core = me % 2
    x = (me // 2) % 4
    z = (me // 8) % 4
    y = me // 32
    cls = (x + y + z) % 4
    head = 2 * cls + core
    line = me // 8
    member = me % 8

    loads = [
        pltpu.make_async_copy(src, dst, load_sem.at[n])
        for n, (src, dst) in enumerate([
            (valid_hbm, valid_ref), (k_hbm, k_ref), (v_hbm, v_ref), (question_hbm, question_ref),
            (q_hbm, q_ref)])
    ]
    for load in loads:
        load.start()

    barrier = pltpu.get_barrier_semaphore()

    def greet(i, carry):
        pl.semaphore_signal(barrier, inc=1, device_id=((me + 1 + i) % N,), device_id_type=MESH)
        return carry

    lax.fori_loop(0, N - 1, greet, 0)

    for load in loads[:4]:
        load.wait()
    valid_here = valid_ref[me]
    row = lax.broadcasted_iota(jnp.int32, (BLK, DH), 0)
    live = row < valid_here
    for h in range(H):
        q64[h:h + 1, :] = question_ref[:, h * DH:(h + 1) * DH].astype(f32)
    for h in range(KVH):
        cols = slice(h * DH, (h + 1) * DH)
        k_h = k_ref[:, cols].astype(f32)
        v_h = v_ref[:, cols].astype(f32)
        kvs[h * 512:h * 512 + 256, :] = jnp.where(live, k_h, k_h[0:1, :]).astype(bf16)
        kvs[h * 512 + 256:h * 512 + 512, :] = jnp.where(live, v_h, 0.0).astype(bf16)
    axis = head % 3
    stride = stride_of(axis)
    first = me - core - ((me // stride) % 4) * stride

    pl.semaphore_wait(barrier, N - 1)

    def send_rows(d, carry):
        other = (head + d) % 8
        target = me - member + ((other // 2 + 8 - y - z) % 4) * 2 + other % 2
        send(q64.at[pl.ds(other * 8, 8)], rows_in.at[member], s_rows, r_rows, target)
        return carry

    lax.fori_loop(1, 8, send_rows, 0)

    @pl.when(me == 0)
    def _():
        def scatter(j, carry):
            send(kvs.at[pl.ds(32 * j, 32)], anchor.at[pl.ds(32 * j, 32)], s_anc.at[0], r_anc.at[0], 2 * j)
            return carry

        def scatter_odd(j, carry):
            piece = 2048 + 32 * (((j // 4) % 4) * 16 + (j % 4) * 4 + j // 16)
            send(kvs.at[pl.ds(piece, 32)], anchor.at[pl.ds(piece, 32)], s_anc.at[5], r_anc.at[0], 2 * j + 1)
            return carry

        lax.fori_loop(0, 64, scatter_odd, 0)
        lax.fori_loop(1, 64, scatter, 0)
        anchor[0:32, :] = kvs[0:32, :]

    def send_kv(d, carry):
        other = (head + d) % 8
        step = stride_of(other % 3)
        at = (me // step) % 4
        target = me - core + ((at + other // 2 + 4 - cls) % 4 - at) * step + other % 2
        send(kvs.at[pl.ds(other * 512, 512)], kvbuf.at[pl.ds((at * 2 + core) * 512, 512)], s_kv, r_kv, target)
        return carry

    at_home = (me // stride) % 4
    own_kv = pltpu.make_async_copy(
        kvs.at[pl.ds(head * 512, 512)], kvbuf.at[pl.ds((at_home * 2 + core) * 512, 512)], own_sem)
    own_kv.start()
    lax.fori_loop(1, 8, send_kv, 0)
    rows_in[member] = q64[pl.ds(head * 8, 8), :]
    for b in range(8):
        valid_b = valid_ref[first + (b // 2) * stride + b % 2]
        ones[b * BLK:(b + 1) * BLK, :] = jnp.where(row < valid_b, 1.0, 0.0).astype(bf16)

    def peer(d):
        other = (line + d) % 16
        return other, peer_device(other)

    def peer_device(other):
        return (other * 4 + (cls + 8 - other // 4 - other % 4) % 4) * 2 + core

    st = (2 + 30 * core, 8 - 6 * core, 32 - 24 * core)
    at = [(me // s) % 4 for s in st]
    half = 2048 * core
    starts = (half + 32 * (at[2] * 16 + at[1] * 4 + at[0]), half + 32 * (at[2] * 16 + at[1] * 4), half + 32 * at[2] * 16)
    sizes = (32, 128, 512)

    def gather_stage(n):
        piece = anchor.at[pl.ds(starts[n], sizes[n])]
        for d in (1, 2, 3):
            target = me + ((at[n] + d) % 4 - at[n]) * st[n]
            send(piece, piece, s_anc.at[n + 1], r_anc.at[n + 1], target)

    def gather_wait(n):
        drain(anchor.at[pl.ds(0, 3 * sizes[n])], r_anc.at[n + 1])

    loads[4].wait()
    causal = lax.broadcasted_iota(jnp.int32, (BLK, BLK), 1) <= lax.broadcasted_iota(jnp.int32, (BLK, BLK), 0)
    ones_own = jnp.where(live, 1.0, 0.0).astype(bf16)

    def own_block(g, carry):
        @pl.when(g == ROWS_AT)
        def _():
            drain(rows_in.at[pl.ds(0, 7)], r_rows)
            q_all[pl.ds(line * 64, 64), :] = rows_in[...].reshape(64, DH).astype(bf16)

            def send_q(d, carry):
                other, target = peer(d)
                send(q_all.at[pl.ds(line * 64, 64)], q_all.at[pl.ds(line * 64, 64)], s_q, r_q, target)
                return carry

            lax.fori_loop(1, 16, send_q, 0)

        base = pl.multiple_of(g * 512, 512)
        keys = kvs[pl.ds(base, 256), :]
        values = jnp.concatenate([kvs[pl.ds(base + 256, 256), :], ones_own], axis=1)
        for h in range(GROUP):
            cols = pl.ds(pl.multiple_of(g * GROUP * DH, GROUP * DH) + h * DH, DH)
            s = lax.dot_general(q_ref[:, cols], keys, NT, preferred_element_type=f32)
            s = jnp.where(causal, s, -1e30)
            peak = jnp.max(s, axis=1, keepdims=True) * EXP2_SCALE
            p = jnp.exp2(s * EXP2_SCALE - peak).astype(bf16)
            o = jnp.dot(p, values, preferred_element_type=f32)
            own_out[:, cols] = o[:, :DH] / o[:, DH:]
            own_lse[:, cols] = peak + jnp.log2(o[:, DH:])
        return carry

    lax.fori_loop(0, KVH, own_block, 0)

    @pl.when(me != 0)
    def _():
        drain(anchor.at[pl.ds(0, 32)], r_anc.at[0])

    gather_stage(0)

    drain(q_all.at[pl.ds(0, 15 * 64)], r_q)
    own_kv.wait()
    drain(kvbuf.at[pl.ds(0, 7 * 512)], r_kv)

    diag = lax.broadcasted_iota(jnp.int32, (64, DH), 0) == lax.broadcasted_iota(jnp.int32, (64, DH), 1)

    def attend(i, carry):
        @pl.when(i == GATHER_1_AT)
        def _():
            gather_wait(0)
            gather_stage(1)

        @pl.when(i == GATHER_2_AT)
        def _():
            gather_wait(1)
            gather_stage(2)

        chunk = (i + line // 2) % 8
        rows = pl.ds(pl.multiple_of(chunk * 128, 128), 128)
        q = q_all[rows, :]
        s = [lax.dot_general(q, kvbuf[b * 512:b * 512 + 256, :], NT, preferred_element_type=f32) for b in range(8)]
        peak = functools.reduce(jnp.maximum, [jnp.max(s_b, axis=1, keepdims=True) for s_b in s]) * EXP2_SCALE
        p = jnp.concatenate([jnp.exp2(s_b * EXP2_SCALE - peak).astype(bf16) for s_b in s], axis=1)
        v = jnp.concatenate(
            [jnp.concatenate([kvbuf[b * 512 + 256:b * 512 + 512, :], ones[b * BLK:(b + 1) * BLK, :]], axis=1) for b in range(8)], axis=0)
        o = jnp.dot(p, v, preferred_element_type=f32)
        total = o[:, DH:]
        part_out[rows, :] = (o[:, :DH] / total).astype(bf16)
        lse = peak + jnp.log2(total)
        for n in range(2):
            other = 2 * chunk + n
            flat = jnp.sum(jnp.where(diag, lse[n * 64:(n + 1) * 64], 0.0), axis=0, keepdims=True)
            lse_out[other] = jnp.broadcast_to(flat, (8, DH))

            @pl.when(other != line)
            def _():
                target = peer_device(other)
                send(part_out.at[pl.ds(other * 64, 64)], part_in.at[pl.ds(line * 64, 64)], s_part, r_part, target)
                send(lse_out.at[other], lse_in.at[line], s_lse, r_lse, target)
        return carry

    lax.fori_loop(0, 8, attend, 0)
    part_in[pl.ds(line * 64, 64), :] = part_out[pl.ds(line * 64, 64), :]
    lse_in[line] = lse_out[line]

    gather_wait(2)
    mine = anchor.at[pl.ds(half, 2048)]
    send(mine, mine, s_anc.at[4], r_anc.at[4], me + 1 - 2 * core)
    ones_first = jnp.where(row < valid_ref[0], 1.0, 0.0).astype(bf16)

    def anchor_block(i, carry):
        g = (4 * core + i) % 8

        @pl.when(i == MERGE_AT)
        def _():
            drain(part_in.at[pl.ds(0, 15 * 64)], r_part)
            drain(lse_in.at[pl.ds(0, 15)], r_lse)
            lse_all = lse_in[...]
            weight = jnp.exp2(lse_all - jnp.max(lse_all, axis=0, keepdims=True))
            weight = weight / jnp.sum(weight, axis=0, keepdims=True)
            merged = jnp.zeros((64, DH), f32)
            for j in range(16):
                column = jnp.sum(jnp.where(diag, weight[j, 0:1, :], 0.0), axis=1, keepdims=True)
                merged += column * part_in[j * 64:(j + 1) * 64, :].astype(f32)
            fin_out[...] = merged.reshape(8, 8, DH)

            def send_fin(d, carry):
                other = (member + d) % 8
                send(fin_out.at[other], fin_in.at[head], s_fin, r_fin, me - member + other)
                return carry

            lax.fori_loop(1, 8, send_fin, 0)
            fin_in[head] = fin_out[member]

        @pl.when(i == 4)
        def _():
            drain(anchor.at[pl.ds(0, 2048)], r_anc.at[4])

        base = pl.multiple_of(g * 512, 512)

        @pl.when(me != 0)
        def _():
            keys = anchor[pl.ds(base, 256), :]
            values = jnp.concatenate([anchor[pl.ds(base + 256, 256), :], ones_first], axis=1)
            for h in range(GROUP):
                cols = pl.ds(pl.multiple_of(g * GROUP * DH, GROUP * DH) + h * DH, DH)
                s = lax.dot_general(q_ref[:, cols], keys, NT, preferred_element_type=f32)
                lse = own_lse[:, cols]
                peak = jnp.maximum(jnp.max(s, axis=1, keepdims=True) * EXP2_SCALE, lse)
                p = jnp.concatenate(
                    [jnp.exp2(s[:, :DH] * EXP2_SCALE - peak), jnp.exp2(s[:, DH:] * EXP2_SCALE - peak)], axis=1).astype(bf16)
                o = jnp.dot(p, values, preferred_element_type=f32)
                scale = jnp.exp2(lse - peak)
                mixed = (o[:, :DH] + scale * own_out[:, cols]) / (o[:, DH:] + scale)
                out_ref[:, cols] = jnp.where(live, mixed, 0.0).astype(bf16)

        @pl.when(me == 0)
        def _():
            for h in range(GROUP):
                cols = pl.ds(pl.multiple_of(g * GROUP * DH, GROUP * DH) + h * DH, DH)
                out_ref[:, cols] = jnp.where(live, own_out[:, cols], 0.0).astype(bf16)

        return carry

    lax.fori_loop(0, KVH, anchor_block, 0)

    drain(fin_in.at[pl.ds(0, 7)], r_fin)
    answer_ref[...] = jnp.where(me < qlen_ref[0], fin_in[...].reshape(64, DH), 0.0)

    drain(rows_in.at[pl.ds(0, 7)], s_rows)
    drain(kvbuf.at[pl.ds(0, 7 * 512)], s_kv)
    drain(q_all.at[pl.ds(0, 15 * 64)], s_q)
    drain(part_in.at[pl.ds(0, 15 * 64)], s_part)
    drain(lse_in.at[pl.ds(0, 15)], s_lse)
    drain(fin_in.at[pl.ds(0, 7)], s_fin)
    for n in range(3):
        drain(anchor.at[pl.ds(0, 3 * sizes[n])], s_anc.at[n + 1])
    drain(anchor.at[pl.ds(0, 2048)], s_anc.at[4])

    @pl.when(me == 0)
    def _():
        drain(anchor.at[pl.ds(0, 63 * 32)], s_anc.at[0])
        drain(anchor.at[pl.ds(0, 2048)], s_anc.at[5])


def body(context_q, context_k, context_v, question, valid, qlen):
    hbm = pl.BlockSpec(memory_space=pltpu.HBM)
    vmem = pl.BlockSpec(memory_space=pltpu.VMEM)
    dma = pltpu.SemaphoreType.DMA
    encoded, answer = pl.pallas_call(
        star_kernel,
        out_shape=(jax.ShapeDtypeStruct((BLK, H * DH), bf16), jax.ShapeDtypeStruct((H, DH), f32)),
        in_specs=[hbm] * 5 + [pl.BlockSpec(memory_space=pltpu.SMEM)],
        out_specs=(vmem, vmem),
        scratch_shapes=[
            pltpu.VMEM((BLK, H * DH), bf16),
            pltpu.VMEM((BLK, KVH * DH), bf16),
            pltpu.VMEM((BLK, KVH * DH), bf16),
            pltpu.VMEM((1, H * DH), bf16),
            pltpu.SMEM((N,), jnp.int32),
            pltpu.VMEM((BLK, H * DH), f32),
            pltpu.VMEM((BLK, H * DH), f32),
            pltpu.VMEM((H, DH), f32),
            pltpu.VMEM((KVH * 512, DH), bf16),
            pltpu.VMEM((8 * 512, DH), bf16),
            pltpu.VMEM((8 * BLK, DH), bf16),
            pltpu.VMEM((8, 8, DH), f32),
            pltpu.VMEM((16 * 64, DH), bf16),
            pltpu.VMEM((16 * 64, DH), bf16),
            pltpu.VMEM((16, 8, DH), f32),
            pltpu.VMEM((16 * 64, DH), bf16),
            pltpu.VMEM((16, 8, DH), f32),
            pltpu.VMEM((8, 8, DH), f32),
            pltpu.VMEM((8, 8, DH), f32),
            pltpu.VMEM((KVH * 512, DH), bf16),
            dma((5,)), dma, dma, dma, dma, dma, dma, dma((6,)), dma((5,)), dma, dma, dma, dma, dma, dma, dma,
        ],
        compiler_params=pltpu.CompilerParams(collective_id=0, has_side_effects=True, vmem_limit_bytes=44 << 20),
        name="star",
    )(*[pltpu.with_memory_space_constraint(a, pltpu.HBM) for a in (context_q, context_k, context_v, question, valid)], qlen)
    return encoded, answer.reshape(1, H * DH).astype(bf16)


def solution(mesh):
    in_specs = (P("ctx", None), P("ctx", None), P("ctx", None), P("ctx", None), P(), P())
    out_specs = (P("ctx", None), P("ctx", None))
    return jax.shard_map(body, mesh=mesh, in_specs=in_specs, out_specs=out_specs, check_vma=False)
```

time: 75.9 us -> 55.2 us (0.73)
  Pallas kernels: 65.8 us -> 51.2 us
  local copies, waits for them, and re-layouts: 8.4 us -> 2.65 us
    pallas_call x2 -> x1, Pallas kernels: 65.8 us -> 51.2 us  [body(): pl.pallas_call(star_kernel, out_shape=(jax.ShapeDtypeStruct((BLK, H * DH)...]
    unnamed x15 -> x2, local copies, waits for them, and re-layouts: 8.4 us -> 2.65 us
where the time goes in v1:
time: 55.2 us; the launch traced here: 55.1 us
  Pallas kernels  51.2 us (93%)
  local copies, waits for them, and re-layouts  2.65 us (5%)
  between operations  1.29 us (2%)
    pallas_call x1, Pallas kernels, body(): pl.pallas_call(star_kernel, out_shape=(jax.ShapeDtypeStruct((BLK, H * DH)...  51.2 us
    unnamed x2, local copies, waits for them, and re-layouts  2.65 us

profile of v1, /device:TPU:1, one launch (start us, length us, event | category | flops | bytes accessed | tf_op | source)
XLA Modules:
  0.0 55.1 jit_solution(10218099646814978814)
XLA Ops:
  1.3 51.2 %star.1 = (bf16[256,8192]{1,0:T(8,128)(2,1)S(1)}, f32[64,128]{1,0:T(8,128)S(1)}) custom-call(bf16[256,8192]{1,0:T(8,128)(2,1)} %q_hbm.1, bf16[256,1024]{1,0:T(8,128)(2,1)} %k_hbm.1, bf16[256,1024]{1,0:T(8,128)(2,1)} %v_hbm.1, bf16[1,8192]{1,0:T(2,128)(2,1)} %question_hbm.1, s32[128]{0:T(128)} %valid_hbm.1, s32[1]{0:T(128)S(6)} %copy.12.qlen_ref), custom_call_target="tpu_custom_call" | custom-call | tf_op jit(solution)/shard_map/star/pallas_call | solution.py:328
  52.5 0.6 %copy.10 = bf16[1,1,64,128]{3,1,2,0:T(2,128)(2,1)} copy(bf16[1,1,64,128]{3,2,1,0:T(8,128)(2,1)S(1)} %convert_bitcast_fusion) | data formatting | bytes 32768
  53.1 2.0 %copy.13 = bf16[256,8192]{1,0:T(8,128)(2,1)} copy(bf16[256,8192]{1,0:T(8,128)(2,1)S(1)} %get-tuple-element.8) | data formatting | bytes 8388608
  (1 shorter events, 0.0 us)

commit v2 on v1

v2 whole, which is shorter than its diff:
```python
import functools

import jax
import jax.numpy as jnp
from jax import lax
from jax.experimental import pallas as pl
from jax.experimental.pallas import tpu as pltpu
from jax.sharding import PartitionSpec as P

H = 64
KVH = 8
DH = 128
BLK = 256
N = 128
GROUP = H // KVH
EXP2_SCALE = 1.4426950408889634 * DH ** (-0.5)

f32 = jnp.float32
bf16 = jnp.bfloat16
MESH = pl.DeviceIdType.MESH
ORDER = (0, 1, 3, 2)
NT = (((1,), (1,)), ((), ()))

ROWS_AT = 1
SPREAD_AT = 2
GATHER_AT = 2
MERGE_AT = 3
GREETINGS = 9 + 1 + 15 + 7 + 7


def stride_of(axis):
    return 2 + 6 * axis + 9 * axis * (axis - 1)


def send(src, dst, send_sem, recv_sem, device):
    pltpu.make_async_remote_copy(
        src_ref=src, dst_ref=dst, send_sem=send_sem, recv_sem=recv_sem,
        device_id=(device,), device_id_type=MESH,
    ).start()


def drain(ref, sem):
    pltpu.make_async_copy(ref, ref, sem).wait()


def star_kernel(
    q_hbm, k_hbm, v_hbm, question_hbm, valid_hbm, qlen_ref,
    out_ref, answer_ref,
    q_ref, k_ref, v_ref, question_ref, valid_ref,
    own_out, own_lse, q64, kvs, kvbuf, ones, rows_in, q_all, part_out, lse_out, part_in, lse_in, fin_out, fin_in, anchor,
    load_sem, s_rows, r_rows, s_q, r_q, s_kv, r_kv, s_anc, r_anc, s_head, r_head, s_core, r_core, s_part, r_part, s_lse, r_lse, s_fin, r_fin, own_sem,
):
    me = lax.axis_index("ctx")
    core = me % 2
    x = (me // 2) % 4
    z = (me // 8) % 4
    y = me // 32
    cls = (x + y + z) % 4
    head = 2 * cls + core
    line = me // 8
    member = me % 8

    loads = [
        pltpu.make_async_copy(src, dst, load_sem.at[n])
        for n, (src, dst) in enumerate([
            (valid_hbm, valid_ref), (k_hbm, k_ref), (v_hbm, v_ref), (question_hbm, question_ref),
            (q_hbm, q_ref)])
    ]
    for load in loads:
        load.start()

    axis = head % 3
    stride = stride_of(axis)
    first = me - core - ((me // stride) % 4) * stride
    other_core = me + 1 - 2 * core

    st = (2 + 30 * core, 8 - 6 * core, 32 - 24 * core)
    at = [(me // step) % 4 for step in st]
    half = 2048 * core

    def along(n, d):
        return me + ((at[n] + d) % 4 - at[n]) * st[n]

    def peer_device(other):
        return (other * 4 + (cls + 8 - other // 4 - other % 4) % 4) * 2 + core

    def peer(d):
        other = (line + d) % 16
        return other, peer_device(other)

    barrier = pltpu.get_barrier_semaphore()

    def greet(device):
        pl.semaphore_signal(barrier, inc=1, device_id=(device,), device_id_type=MESH)

    @pl.when(jnp.logical_and(at[0] == 0, me != 0))
    def _():
        greet(0)

    for n in range(3):
        for d in (1, 2, 3):
            greet(along(n, d))
    greet(other_core)
    for d in range(1, 16):
        greet(peer(d)[1])
    for d in range(1, 8):
        greet(me - member + (member + d) % 8)
        source = ((me // stride) % 4 * 2 + core + d) % 8
        greet(first + source // 2 * stride + source % 2)

    for load in loads[:4]:
        load.wait()
    valid_here = valid_ref[me]
    row = lax.broadcasted_iota(jnp.int32, (BLK, DH), 0)
    live = row < valid_here
    for h in range(H):
        q64[h:h + 1, :] = question_ref[:, h * DH:(h + 1) * DH].astype(f32)
    for h in range(KVH):
        cols = slice(h * DH, (h + 1) * DH)
        k_h = k_ref[:, cols].astype(f32)
        v_h = v_ref[:, cols].astype(f32)
        kvs[h * 512:h * 512 + 256, :] = jnp.where(live, k_h, k_h[0:1, :]).astype(bf16)
        kvs[h * 512 + 256:h * 512 + 512, :] = jnp.where(live, v_h, 0.0).astype(bf16)
    @pl.when(me == 0)
    def _():
        pl.semaphore_wait(barrier, GREETINGS + 31)

    @pl.when(me != 0)
    def _():
        pl.semaphore_wait(barrier, GREETINGS)

    def send_rows(d, carry):
        other = (head + d) % 8
        target = me - member + ((other // 2 + 8 - y - z) % 4) * 2 + other % 2
        send(q64.at[pl.ds(other * 8, 8)], rows_in.at[member], s_rows, r_rows, target)
        return carry

    lax.fori_loop(1, 8, send_rows, 0)

    @pl.when(me == 0)
    def _():
        def scatter(j, carry):
            piece = 2048 + 128 * ((j % 4) * 4 + j // 4)
            send(kvs.at[pl.ds(piece, 128)], anchor.at[pl.ds(piece, 128)], s_anc.at[0], r_anc.at[0], 8 * (j % 4) + 2 * (j // 4) + 1)

            @pl.when(j != 0)
            def _():
                piece = 128 * j
                send(kvs.at[pl.ds(piece, 128)], anchor.at[pl.ds(piece, 128)], s_anc.at[3], r_anc.at[0], 8 * j)

            return carry

        lax.fori_loop(0, 16, scatter, 0)
        anchor[0:128, :] = kvs[0:128, :]

    def send_kv(d, carry):
        other = (head + d) % 8
        step = stride_of(other % 3)
        at = (me // step) % 4
        target = me - core + ((at + other // 2 + 4 - cls) % 4 - at) * step + other % 2
        send(kvs.at[pl.ds(other * 512, 512)], kvbuf.at[pl.ds((at * 2 + core) * 512, 512)], s_kv, r_kv, target)
        return carry

    at_home = (me // stride) % 4
    own_kv = pltpu.make_async_copy(
        kvs.at[pl.ds(head * 512, 512)], kvbuf.at[pl.ds((at_home * 2 + core) * 512, 512)], own_sem)
    own_kv.start()
    lax.fori_loop(1, 8, send_kv, 0)
    rows_in[member] = q64[pl.ds(head * 8, 8), :]
    for b in range(8):
        valid_b = valid_ref[first + (b // 2) * stride + b % 2]
        ones[b * BLK:(b + 1) * BLK, :] = jnp.where(row < valid_b, 1.0, 0.0).astype(bf16)

    spread_rows = pl.ds(half + 512 * at[2] + 128 * at[1], 128)

    def spread():
        @pl.when(at[0] == 0)
        def _():
            @pl.when(me != 0)
            def _():
                drain(anchor.at[pl.ds(0, 128)], r_anc.at[0])

            for d in (1, 2, 3):
                send(anchor.at[spread_rows], anchor.at[spread_rows], s_anc.at[1], r_anc.at[1], along(0, d))
            send_gather()

    def gather():
        @pl.when(at[0] != 0)
        def _():
            drain(anchor.at[pl.ds(0, 128)], r_anc.at[1])
            send_gather()

    def send_gather():
        for d in (1, 2, 3):
            send(anchor.at[spread_rows], anchor.at[spread_rows], s_anc.at[2], r_anc.at[2], along(1, d))

    def own_head(j):
        return 4 * core + (at[2] + ORDER[j]) % 4

    def share(j):
        rows = anchor.at[pl.ds(own_head(j) * 512, 512)]
        send(rows, rows, s_core.at[j], r_core.at[j], other_core)

    def gather_heads():
        drain(anchor.at[pl.ds(0, 3 * 128)], r_anc.at[2])
        share(0)
        rows = anchor.at[pl.ds(own_head(0) * 512, 512)]
        for j in (1, 2, 3):
            send(rows, rows, s_head.at[j], r_head.at[j], along(2, 4 - ORDER[j]))

    def pass_on(j):
        drain(anchor.at[pl.ds(0, 512)], r_head.at[j])
        share(j)

    loads[4].wait()
    causal = lax.broadcasted_iota(jnp.int32, (BLK, BLK), 1) <= lax.broadcasted_iota(jnp.int32, (BLK, BLK), 0)
    ones_own = jnp.where(live, 1.0, 0.0).astype(bf16)

    def own_block(n, carry):
        @pl.when(n == ROWS_AT)
        def _():
            drain(rows_in.at[pl.ds(0, 7)], r_rows)
            q_all[pl.ds(line * 64, 64), :] = rows_in[...].reshape(64, DH).astype(bf16)

            def send_q(d, carry):
                other, target = peer(d)
                send(q_all.at[pl.ds(line * 64, 64)], q_all.at[pl.ds(line * 64, 64)], s_q, r_q, target)
                return carry

            lax.fori_loop(1, 16, send_q, 0)

        pl.when(n == SPREAD_AT)(spread)
        for g in (2 * n, 2 * n + 1):
            base = pl.multiple_of(g * 512, 512)
            keys = kvs[pl.ds(base, 256), :]
            values = jnp.concatenate([kvs[pl.ds(base + 256, 256), :], ones_own], axis=1)
            for h in range(GROUP):
                cols = pl.ds(pl.multiple_of(g * GROUP * DH, GROUP * DH) + h * DH, DH)
                s = lax.dot_general(q_ref[:, cols], keys, NT, preferred_element_type=f32)
                s = jnp.where(causal, s, -1e30)
                peak = jnp.max(s, axis=1, keepdims=True) * EXP2_SCALE
                p = jnp.exp2(s * EXP2_SCALE - peak).astype(bf16)
                o = jnp.dot(p, values, preferred_element_type=f32)
                own_out[:, cols] = o[:, :DH] / o[:, DH:]
                own_lse[:, cols] = peak + jnp.log2(o[:, DH:])
        return carry

    lax.fori_loop(0, KVH // 2, own_block, 0)

    gather()

    drain(q_all.at[pl.ds(0, 15 * 64)], r_q)
    own_kv.wait()
    drain(kvbuf.at[pl.ds(0, 7 * 512)], r_kv)

    diag = lax.broadcasted_iota(jnp.int32, (64, DH), 0) == lax.broadcasted_iota(jnp.int32, (64, DH), 1)

    def attend(i, carry):
        pl.when(i == GATHER_AT)(gather_heads)
        chunk = (i + line // 4) % 4
        rows = pl.ds(pl.multiple_of(chunk * 256, 256), 256)
        q = q_all[rows, :]
        peak = None
        for b in range(0, 8, 2):
            keys = jnp.concatenate([kvbuf[n * 512:n * 512 + 256, :] for n in (b, b + 1)], axis=0)
            values = jnp.concatenate(
                [jnp.concatenate([kvbuf[n * 512 + 256:n * 512 + 512, :], ones[n * BLK:(n + 1) * BLK, :]], axis=1) for n in (b, b + 1)],
                axis=0)
            s = lax.dot_general(q, keys, NT, preferred_element_type=f32)
            new_peak = jnp.max(s, axis=1, keepdims=True) * EXP2_SCALE
            if peak is not None:
                new_peak = jnp.maximum(peak, new_peak)
            p = jnp.exp2(s * EXP2_SCALE - new_peak).astype(bf16)
            o_b = jnp.dot(p, values, preferred_element_type=f32)
            o = o_b if peak is None else o * jnp.exp2(peak - new_peak) + o_b
            peak = new_peak
        total = o[:, DH:]
        part_out[rows, :] = (o[:, :DH] / total).astype(bf16)
        lse = peak + jnp.log2(total)
        for n in range(4):
            other = 4 * chunk + n
            flat = jnp.sum(jnp.where(diag, lse[n * 64:(n + 1) * 64], 0.0), axis=0, keepdims=True)
            lse_out[other] = jnp.broadcast_to(flat, (8, DH))

            @pl.when(other != line)
            def _():
                target = peer_device(other)
                send(part_out.at[pl.ds(other * 64, 64)], part_in.at[pl.ds(line * 64, 64)], s_part, r_part, target)
                send(lse_out.at[other], lse_in.at[line], s_lse, r_lse, target)
        return carry

    lax.fori_loop(0, 4, attend, 0)
    part_in[pl.ds(line * 64, 64), :] = part_out[pl.ds(line * 64, 64), :]
    lse_in[line] = lse_out[line]

    ones_first = jnp.where(row < valid_ref[0], 1.0, 0.0).astype(bf16)

    def anchor_block(i, carry):
        is_1, is_2, is_3 = i * (2 - i) * (3 - i) // 2, i * (i - 1) * (3 - i) // 2, i * (i - 1) * (i - 2) // 6
        core_a, core_b = (core + is_2) % 2, (core + 1 - is_1) % 2
        far_a, far_b = is_1 + is_2 + 2 * is_3, 3 * (is_1 + is_2) + 2 * is_3

        def head_at(c, far):
            return 4 * c + (c * z + (1 - c) * y + far) % 4

        @pl.when(i == 0)
        def _():
            drain(anchor.at[pl.ds(0, 512)], r_core.at[0])

        @pl.when(i == 1)
        def _():
            pass_on(1)
            pass_on(2)

        @pl.when(i == 2)
        def _():
            pass_on(3)
            drain(anchor.at[pl.ds(0, 512)], r_core.at[1])
            drain(anchor.at[pl.ds(0, 512)], r_core.at[2])

        @pl.when(i == 3)
        def _():
            drain(anchor.at[pl.ds(0, 512)], r_core.at[3])

        @pl.when(i == MERGE_AT)
        def _():
            drain(part_in.at[pl.ds(0, 15 * 64)], r_part)
            drain(lse_in.at[pl.ds(0, 15)], r_lse)
            lse_all = lse_in[...]
            weight = jnp.exp2(lse_all - jnp.max(lse_all, axis=0, keepdims=True))
            weight = weight / jnp.sum(weight, axis=0, keepdims=True)
            merged = jnp.zeros((64, DH), f32)
            for j in range(16):
                column = jnp.sum(jnp.where(diag, weight[j, 0:1, :], 0.0), axis=1, keepdims=True)
                merged += column * part_in[j * 64:(j + 1) * 64, :].astype(f32)
            fin_out[...] = merged.reshape(8, 8, DH)

            def send_fin(d, carry):
                other = (member + d) % 8
                send(fin_out.at[other], fin_in.at[head], s_fin, r_fin, me - member + other)
                return carry

            lax.fori_loop(1, 8, send_fin, 0)
            fin_in[head] = fin_out[member]

        groups = (head_at(core_a, far_a), head_at(core_b, far_b))

        @pl.when(me != 0)
        def _():
            for g in groups:
                base = pl.multiple_of(g * 512, 512)
                keys = anchor[pl.ds(base, 256), :]
                values = jnp.concatenate([anchor[pl.ds(base + 256, 256), :], ones_first], axis=1)
                for h in range(GROUP):
                    cols = pl.ds(pl.multiple_of(g * GROUP * DH, GROUP * DH) + h * DH, DH)
                    s = lax.dot_general(q_ref[:, cols], keys, NT, preferred_element_type=f32)
                    lse = own_lse[:, cols]
                    peak = jnp.maximum(jnp.max(s, axis=1, keepdims=True) * EXP2_SCALE, lse)
                    p = jnp.concatenate(
                        [jnp.exp2(s[:, :DH] * EXP2_SCALE - peak), jnp.exp2(s[:, DH:] * EXP2_SCALE - peak)], axis=1).astype(bf16)
                    o = jnp.dot(p, values, preferred_element_type=f32)
                    scale = jnp.exp2(lse - peak)
                    mixed = (o[:, :DH] + scale * own_out[:, cols]) / (o[:, DH:] + scale)
                    out_ref[:, cols] = jnp.where(live, mixed, 0.0).astype(bf16)

        @pl.when(me == 0)
        def _():
            for g in groups:
                for h in range(GROUP):
                    cols = pl.ds(pl.multiple_of(g * GROUP * DH, GROUP * DH) + h * DH, DH)
                    out_ref[:, cols] = jnp.where(live, own_out[:, cols], 0.0).astype(bf16)

        return carry

    lax.fori_loop(0, KVH // 2, anchor_block, 0)

    drain(fin_in.at[pl.ds(0, 7)], r_fin)
    answer_ref[...] = jnp.where(me < qlen_ref[0], fin_in[...].reshape(64, DH), 0.0)

    drain(rows_in.at[pl.ds(0, 7)], s_rows)
    drain(kvbuf.at[pl.ds(0, 7 * 512)], s_kv)
    drain(q_all.at[pl.ds(0, 15 * 64)], s_q)
    drain(part_in.at[pl.ds(0, 15 * 64)], s_part)
    drain(lse_in.at[pl.ds(0, 15)], s_lse)
    drain(fin_in.at[pl.ds(0, 7)], s_fin)
    drain(anchor.at[pl.ds(0, 3 * 128)], s_anc.at[2])
    for n in range(4):
        drain(anchor.at[pl.ds(0, 512)], s_core.at[n])
    for n in range(1, 4):
        drain(anchor.at[pl.ds(0, 512)], s_head.at[n])

    @pl.when(at[0] == 0)
    def _():
        drain(anchor.at[pl.ds(0, 3 * 128)], s_anc.at[1])

    @pl.when(me == 0)
    def _():
        drain(anchor.at[pl.ds(0, 2048)], s_anc.at[0])
        drain(anchor.at[pl.ds(0, 15 * 128)], s_anc.at[3])


def body(context_q, context_k, context_v, question, valid, qlen):
    hbm = pl.BlockSpec(memory_space=pltpu.HBM)
    vmem = pl.BlockSpec(memory_space=pltpu.VMEM)
    dma = pltpu.SemaphoreType.DMA
    encoded, answer = pl.pallas_call(
        star_kernel,
        out_shape=(jax.ShapeDtypeStruct((BLK, H * DH), bf16), jax.ShapeDtypeStruct((H, DH), f32)),
        in_specs=[hbm] * 5 + [pl.BlockSpec(memory_space=pltpu.SMEM)],
        out_specs=(vmem, vmem),
        scratch_shapes=[
            pltpu.VMEM((BLK, H * DH), bf16),
            pltpu.VMEM((BLK, KVH * DH), bf16),
            pltpu.VMEM((BLK, KVH * DH), bf16),
            pltpu.VMEM((1, H * DH), bf16),
            pltpu.SMEM((N,), jnp.int32),
            pltpu.VMEM((BLK, H * DH), f32),
            pltpu.VMEM((BLK, H * DH), f32),
            pltpu.VMEM((H, DH), f32),
            pltpu.VMEM((KVH * 512, DH), bf16),
            pltpu.VMEM((8 * 512, DH), bf16),
            pltpu.VMEM((8 * BLK, DH), bf16),
            pltpu.VMEM((8, 8, DH), f32),
            pltpu.VMEM((16 * 64, DH), bf16),
            pltpu.VMEM((16 * 64, DH), bf16),
            pltpu.VMEM((16, 8, DH), f32),
            pltpu.VMEM((16 * 64, DH), bf16),
            pltpu.VMEM((16, 8, DH), f32),
            pltpu.VMEM((8, 8, DH), f32),
            pltpu.VMEM((8, 8, DH), f32),
            pltpu.VMEM((KVH * 512, DH), bf16),
            dma((5,)), dma, dma, dma, dma, dma, dma, dma((4,)), dma((3,)), dma((4,)), dma((4,)), dma((4,)), dma((4,)), dma, dma, dma, dma, dma, dma, dma,
        ],
        compiler_params=pltpu.CompilerParams(collective_id=0, has_side_effects=True, vmem_limit_bytes=44 << 20),
        name="star",
    )(*[pltpu.with_memory_space_constraint(a, pltpu.HBM) for a in (context_q, context_k, context_v, question, valid)], qlen)
    return encoded, answer.reshape(1, H * DH).astype(bf16)


def solution(mesh):
    in_specs = (P("ctx", None), P("ctx", None), P("ctx", None), P("ctx", None), P(), P())
    out_specs = (P("ctx", None), P("ctx", None))
    return jax.shard_map(body, mesh=mesh, in_specs=in_specs, out_specs=out_specs, check_vma=False)
```

time: 55.2 us -> 46.9 us (0.85)
  Pallas kernels: 51.2 us -> 42.8 us
    pallas_call x1, Pallas kernels: 51.2 us -> 42.8 us  [body(): pl.pallas_call(star_kernel, out_shape=(jax.ShapeDtypeStruct((BLK, H * DH)...]
where the time goes in v2:
time: 46.9 us; the launch traced here: 46.7 us
  Pallas kernels  42.8 us (91%)
  local copies, waits for them, and re-layouts  2.65 us (6%)
  between operations  1.29 us (3%)
    pallas_call x1, Pallas kernels, body(): pl.pallas_call(star_kernel, out_shape=(jax.ShapeDtypeStruct((BLK, H * DH)...  42.8 us
    unnamed x2, local copies, waits for them, and re-layouts  2.65 us

profile of v2, /device:TPU:1, one launch (start us, length us, event | category | flops | bytes accessed | tf_op | source)
XLA Modules:
  0.0 46.7 jit_solution(9703521343704860888)
XLA Ops:
  1.3 42.8 %star.1 = (bf16[256,8192]{1,0:T(8,128)(2,1)S(1)}, f32[64,128]{1,0:T(8,128)S(1)}) custom-call(bf16[256,8192]{1,0:T(8,128)(2,1)} %q_hbm.1, bf16[256,1024]{1,0:T(8,128)(2,1)} %k_hbm.1, bf16[256,1024]{1,0:T(8,128)(2,1)} %v_hbm.1, bf16[1,8192]{1,0:T(2,128)(2,1)} %question_hbm.1, s32[128]{0:T(128)} %valid_hbm.1, s32[1]{0:T(128)S(6)} %copy.12.qlen_ref), custom_call_target="tpu_custom_call" | custom-call | tf_op jit(solution)/shard_map/star/pallas_call | solution.py:406
  44.1 0.6 %copy.10 = bf16[1,1,64,128]{3,1,2,0:T(2,128)(2,1)} copy(bf16[1,1,64,128]{3,2,1,0:T(8,128)(2,1)S(1)} %convert_bitcast_fusion) | data formatting | bytes 32768
  44.7 2.0 %copy.13 = bf16[256,8192]{1,0:T(8,128)(2,1)} copy(bf16[256,8192]{1,0:T(8,128)(2,1)S(1)} %get-tuple-element.8) | data formatting | bytes 8388608
  (1 shorter events, 0.0 us)

commit v3 on v2

--- a/solution.py
+++ b/solution.py
@@ -21,10 +21,10 @@
 ORDER = (0, 1, 3, 2)
 NT = (((1,), (1,)), ((), ()))
 
-ROWS_AT = 1
+ROWS_AT = 2
 SPREAD_AT = 2
 GATHER_AT = 2
-MERGE_AT = 3
+MERGE_AT = 2
 GREETINGS = 9 + 1 + 15 + 7 + 7
 
 
@@ -60,15 +60,6 @@
     line = me // 8
     member = me % 8
 
-    loads = [
-        pltpu.make_async_copy(src, dst, load_sem.at[n])
-        for n, (src, dst) in enumerate([
-            (valid_hbm, valid_ref), (k_hbm, k_ref), (v_hbm, v_ref), (question_hbm, question_ref),
-            (q_hbm, q_ref)])
-    ]
-    for load in loads:
-        load.start()
-
     axis = head % 3
     stride = stride_of(axis)
     first = me - core - ((me // stride) % 4) * stride
@@ -107,6 +98,15 @@
         greet(me - member + (member + d) % 8)
         source = ((me // stride) % 4 * 2 + core + d) % 8
         greet(first + source // 2 * stride + source % 2)
+
+    loads = [
+        pltpu.make_async_copy(src, dst, load_sem.at[n])
+        for n, (src, dst) in enumerate([
+            (valid_hbm, valid_ref), (k_hbm, k_ref), (v_hbm, v_ref), (question_hbm, question_ref),
+            (q_hbm, q_ref)])
+    ]
+    for load in loads:
+        load.start()
 
     for load in loads[:4]:
         load.wait()
@@ -137,9 +137,51 @@
 
     lax.fori_loop(1, 8, send_rows, 0)
 
+    spread_rows = pl.ds(half + 512 * at[2] + 128 * at[1], 128)
+
+    def send_spread():
+        for d in (1, 2, 3):
+            send(anchor.at[spread_rows], anchor.at[spread_rows], s_anc.at[1], r_anc.at[1], along(0, d))
+        send_gather()
+
+    def spread():
+        @pl.when(jnp.logical_and(at[0] == 0, me != 0))
+        def _():
+            drain(anchor.at[pl.ds(0, 128)], r_anc.at[0])
+            send_spread()
+
+    def gather():
+        @pl.when(at[0] != 0)
+        def _():
+            drain(anchor.at[pl.ds(0, 128)], r_anc.at[1])
+            send_gather()
+
+    def send_gather():
+        for d in (1, 2, 3):
+            send(anchor.at[spread_rows], anchor.at[spread_rows], s_anc.at[2], r_anc.at[2], along(1, d))
+
+    def own_head(j):
+        return 4 * core + (at[2] + ORDER[j]) % 4
+
+    def share(j):
+        rows = anchor.at[pl.ds(own_head(j) * 512, 512)]
+        send(rows, rows, s_core.at[j], r_core.at[j], other_core)
+
+    def gather_heads():
+        drain(anchor.at[pl.ds(0, 3 * 128)], r_anc.at[2])
+        share(0)
+        rows = anchor.at[pl.ds(own_head(0) * 512, 512)]
+        for j in (1, 2, 3):
+            send(rows, rows, s_head.at[j], r_head.at[j], along(2, 4 - ORDER[j]))
+
+    def pass_on(j):
+        drain(anchor.at[pl.ds(0, 512)], r_head.at[j])
+        share(j)
+
     @pl.when(me == 0)
     def _():
-        def scatter(j, carry):
+        def scatter(i, carry):
+            j = (i % 4) * 4 + (2 + 3 * (i // 4)) % 4
             piece = 2048 + 128 * ((j % 4) * 4 + j // 4)
             send(kvs.at[pl.ds(piece, 128)], anchor.at[pl.ds(piece, 128)], s_anc.at[0], r_anc.at[0], 8 * (j % 4) + 2 * (j // 4) + 1)
 
@@ -150,8 +192,9 @@
 
             return carry
 
+        anchor[0:128, :] = kvs[0:128, :]
         lax.fori_loop(0, 16, scatter, 0)
-        anchor[0:128, :] = kvs[0:128, :]
+        send_spread()
 
     def send_kv(d, carry):
         other = (head + d) % 8
@@ -165,58 +208,23 @@
     own_kv = pltpu.make_async_copy(
         kvs.at[pl.ds(head * 512, 512)], kvbuf.at[pl.ds((at_home * 2 + core) * 512, 512)], own_sem)
     own_kv.start()
-    lax.fori_loop(1, 8, send_kv, 0)
+    @pl.when(me > 1)
+    def _():
+        lax.fori_loop(1, 8, send_kv, 0)
+
     rows_in[member] = q64[pl.ds(head * 8, 8), :]
     for b in range(8):
         valid_b = valid_ref[first + (b // 2) * stride + b % 2]
         ones[b * BLK:(b + 1) * BLK, :] = jnp.where(row < valid_b, 1.0, 0.0).astype(bf16)
 
-    spread_rows = pl.ds(half + 512 * at[2] + 128 * at[1], 128)
-
-    def spread():
-        @pl.when(at[0] == 0)
-        def _():
-            @pl.when(me != 0)
-            def _():
-                drain(anchor.at[pl.ds(0, 128)], r_anc.at[0])
-
-            for d in (1, 2, 3):
-                send(anchor.at[spread_rows], anchor.at[spread_rows], s_anc.at[1], r_anc.at[1], along(0, d))
-            send_gather()
-
-    def gather():
-        @pl.when(at[0] != 0)
-        def _():
-            drain(anchor.at[pl.ds(0, 128)], r_anc.at[1])
-            send_gather()
-
-    def send_gather():
-        for d in (1, 2, 3):
-            send(anchor.at[spread_rows], anchor.at[spread_rows], s_anc.at[2], r_anc.at[2], along(1, d))
-
-    def own_head(j):
-        return 4 * core + (at[2] + ORDER[j]) % 4
-
-    def share(j):
-        rows = anchor.at[pl.ds(own_head(j) * 512, 512)]
-        send(rows, rows, s_core.at[j], r_core.at[j], other_core)
-
-    def gather_heads():
-        drain(anchor.at[pl.ds(0, 3 * 128)], r_anc.at[2])
-        share(0)
-        rows = anchor.at[pl.ds(own_head(0) * 512, 512)]
-        for j in (1, 2, 3):
-            send(rows, rows, s_head.at[j], r_head.at[j], along(2, 4 - ORDER[j]))
-
-    def pass_on(j):
-        drain(anchor.at[pl.ds(0, 512)], r_head.at[j])
-        share(j)
-
     loads[4].wait()
     causal = lax.broadcasted_iota(jnp.int32, (BLK, BLK), 1) <= lax.broadcasted_iota(jnp.int32, (BLK, BLK), 0)
     ones_own = jnp.where(live, 1.0, 0.0).astype(bf16)
 
     def own_block(n, carry):
+
+        pl.when(n == SPREAD_AT)(spread)
+
         @pl.when(n == ROWS_AT)
         def _():
             drain(rows_in.at[pl.ds(0, 7)], r_rows)
@@ -224,12 +232,18 @@
 
             def send_q(d, carry):
                 other, target = peer(d)
-                send(q_all.at[pl.ds(line * 64, 64)], q_all.at[pl.ds(line * 64, 64)], s_q, r_q, target)
+                send(q_all.at[pl.ds(line * 64, 64)], q_all.at[pl.ds(line * 64, 64)], s_q, r_q.at[y], target)
                 return carry
 
             lax.fori_loop(1, 16, send_q, 0)
 
-        pl.when(n == SPREAD_AT)(spread)
+
+        @pl.when(n == 2)
+        def _():
+            @pl.when(me <= 1)
+            def _():
+                lax.fori_loop(1, 8, send_kv, 0)
+
         for g in (2 * n, 2 * n + 1):
             base = pl.multiple_of(g * 512, 512)
             keys = kvs[pl.ds(base, 256), :]
@@ -241,7 +255,7 @@
                 peak = jnp.max(s, axis=1, keepdims=True) * EXP2_SCALE
                 p = jnp.exp2(s * EXP2_SCALE - peak).astype(bf16)
                 o = jnp.dot(p, values, preferred_element_type=f32)
-                own_out[:, cols] = o[:, :DH] / o[:, DH:]
+                own_out[:, cols] = o[:, :DH] * pl.reciprocal(o[:, DH:], approx=True)
                 own_lse[:, cols] = peak + jnp.log2(o[:, DH:])
         return carry
 
@@ -249,7 +263,6 @@
 
     gather()
 
-    drain(q_all.at[pl.ds(0, 15 * 64)], r_q)
     own_kv.wait()
     drain(kvbuf.at[pl.ds(0, 7 * 512)], r_kv)
 
@@ -257,7 +270,16 @@
 
     def attend(i, carry):
         pl.when(i == GATHER_AT)(gather_heads)
-        chunk = (i + line // 4) % 4
+        chunk = (i + y) % 4
+
+        @pl.when(i == 0)
+        def _():
+            drain(q_all.at[pl.ds(0, 3 * 64)], r_q.at[chunk])
+
+        @pl.when(i != 0)
+        def _():
+            drain(q_all.at[pl.ds(0, 4 * 64)], r_q.at[chunk])
+
         rows = pl.ds(pl.multiple_of(chunk * 256, 256), 256)
         q = q_all[rows, :]
         peak = None
@@ -275,7 +297,7 @@
             o = o_b if peak is None else o * jnp.exp2(peak - new_peak) + o_b
             peak = new_peak
         total = o[:, DH:]
-        part_out[rows, :] = (o[:, :DH] / total).astype(bf16)
+        part_out[rows, :] = (o[:, :DH] * pl.reciprocal(total, approx=True)).astype(bf16)
         lse = peak + jnp.log2(total)
         for n in range(4):
             other = 4 * chunk + n
@@ -360,7 +382,7 @@
                         [jnp.exp2(s[:, :DH] * EXP2_SCALE - peak), jnp.exp2(s[:, DH:] * EXP2_SCALE - peak)], axis=1).astype(bf16)
                     o = jnp.dot(p, values, preferred_element_type=f32)
                     scale = jnp.exp2(lse - peak)
-                    mixed = (o[:, :DH] + scale * own_out[:, cols]) / (o[:, DH:] + scale)
+                    mixed = (o[:, :DH] + scale * own_out[:, cols]) * pl.reciprocal(o[:, DH:] + scale, approx=True)
                     out_ref[:, cols] = jnp.where(live, mixed, 0.0).astype(bf16)
 
         @pl.when(me == 0)
@@ -429,7 +451,7 @@
             pltpu.VMEM((8, 8, DH), f32),
             pltpu.VMEM((8, 8, DH), f32),
             pltpu.VMEM((KVH * 512, DH), bf16),
-            dma((5,)), dma, dma, dma, dma, dma, dma, dma((4,)), dma((3,)), dma((4,)), dma((4,)), dma((4,)), dma((4,)), dma, dma, dma, dma, dma, dma, dma,
+            dma((5,)), dma, dma, dma, dma((4,)), dma, dma, dma((4,)), dma((3,)), dma((4,)), dma((4,)), dma((4,)), dma((4,)), dma, dma, dma, dma, dma, dma, dma,
         ],
         compiler_params=pltpu.CompilerParams(collective_id=0, has_side_effects=True, vmem_limit_bytes=44 << 20),
         name="star",

time: 46.9 us -> 42.9 us (0.915)
  Pallas kernels: 42.8 us -> 38.8 us
    pallas_call x1, Pallas kernels: 42.8 us -> 38.8 us  [body(): pl.pallas_call(star_kernel, out_shape=(jax.ShapeDtypeStruct((BLK, H * DH)...]
where the time goes in v3:
time: 42.9 us; the launch traced here: 42.8 us
  Pallas kernels  38.8 us (90%)
  local copies, waits for them, and re-layouts  2.65 us (6%)
  between operations  1.29 us (3%)
    pallas_call x1, Pallas kernels, body(): pl.pallas_call(star_kernel, out_shape=(jax.ShapeDtypeStruct((BLK, H * DH)...  38.8 us
    unnamed x2, local copies, waits for them, and re-layouts  2.65 us

profile of v3, /device:TPU:1, one launch (start us, length us, event | category | flops | bytes accessed | tf_op | source)
XLA Modules:
  0.0 42.8 jit_solution(8987552435531390108)
XLA Ops:
  1.3 38.8 %star.1 = (bf16[256,8192]{1,0:T(8,128)(2,1)S(1)}, f32[64,128]{1,0:T(8,128)S(1)}) custom-call(bf16[256,8192]{1,0:T(8,128)(2,1)} %q_hbm.1, bf16[256,1024]{1,0:T(8,128)(2,1)} %k_hbm.1, bf16[256,1024]{1,0:T(8,128)(2,1)} %v_hbm.1, bf16[1,8192]{1,0:T(2,128)(2,1)} %question_hbm.1, s32[128]{0:T(128)} %valid_hbm.1, s32[1]{0:T(128)S(6)} %copy.12.qlen_ref), custom_call_target="tpu_custom_call" | custom-call | tf_op jit(solution)/shard_map/star/pallas_call | solution.py:428
  40.1 0.6 %copy.10 = bf16[1,1,64,128]{3,1,2,0:T(2,128)(2,1)} copy(bf16[1,1,64,128]{3,2,1,0:T(8,128)(2,1)S(1)} %convert_bitcast_fusion) | data formatting | bytes 32768
  40.8 2.0 %copy.13 = bf16[256,8192]{1,0:T(8,128)(2,1)} copy(bf16[256,8192]{1,0:T(8,128)(2,1)S(1)} %get-tuple-element.8) | data formatting | bytes 8388608
  (1 shorter events, 0.0 us)

commit v4 on v3

--- a/solution.py
+++ b/solution.py
@@ -18,6 +18,7 @@
 f32 = jnp.float32
 bf16 = jnp.bfloat16
 MESH = pl.DeviceIdType.MESH
+DEAD = 1e30
 ORDER = (0, 1, 3, 2)
 NT = (((1,), (1,)), ((), ()))
 
@@ -181,7 +182,7 @@
     @pl.when(me == 0)
     def _():
         def scatter(i, carry):
-            j = (i % 4) * 4 + (2 + 3 * (i // 4)) % 4
+            j = ((i + 2) % 4) * 4 + (2 + 3 * (i // 4)) % 4
             piece = 2048 + 128 * ((j % 4) * 4 + j // 4)
             send(kvs.at[pl.ds(piece, 128)], anchor.at[pl.ds(piece, 128)], s_anc.at[0], r_anc.at[0], 8 * (j % 4) + 2 * (j // 4) + 1)
 
@@ -255,8 +256,8 @@
                 peak = jnp.max(s, axis=1, keepdims=True) * EXP2_SCALE
                 p = jnp.exp2(s * EXP2_SCALE - peak).astype(bf16)
                 o = jnp.dot(p, values, preferred_element_type=f32)
-                own_out[:, cols] = o[:, :DH] * pl.reciprocal(o[:, DH:], approx=True)
-                own_lse[:, cols] = peak + jnp.log2(o[:, DH:])
+                own_out[:, cols] = jnp.where(live, o[:, :DH] * pl.reciprocal(o[:, DH:], approx=True), 0.0)
+                own_lse[:, cols] = jnp.where(live, peak + jnp.log2(o[:, DH:]), DEAD)
         return carry
 
     lax.fori_loop(0, KVH // 2, own_block, 0)
@@ -383,14 +384,14 @@
                     o = jnp.dot(p, values, preferred_element_type=f32)
                     scale = jnp.exp2(lse - peak)
                     mixed = (o[:, :DH] + scale * own_out[:, cols]) * pl.reciprocal(o[:, DH:] + scale, approx=True)
-                    out_ref[:, cols] = jnp.where(live, mixed, 0.0).astype(bf16)
+                    out_ref[:, cols] = mixed.astype(bf16)
 
         @pl.when(me == 0)
         def _():
             for g in groups:
                 for h in range(GROUP):
                     cols = pl.ds(pl.multiple_of(g * GROUP * DH, GROUP * DH) + h * DH, DH)
-                    out_ref[:, cols] = jnp.where(live, own_out[:, cols], 0.0).astype(bf16)
+                    out_ref[:, cols] = own_out[:, cols].astype(bf16)
 
         return carry
 

time: 42.9 us -> 42.4 us (0.988)
    pallas_call x1, Pallas kernels: 38.8 us -> 38.4 us  [body(): pl.pallas_call(star_kernel, out_shape=(jax.ShapeDtypeStruct((BLK, H * DH)...]
where the time goes in v4:
time: 42.4 us; the launch traced here: 42.3 us
  Pallas kernels  38.4 us (91%)
  local copies, waits for them, and re-layouts  2.65 us (6%)
  between operations  1.29 us (3%)
    pallas_call x1, Pallas kernels, body(): pl.pallas_call(star_kernel, out_shape=(jax.ShapeDtypeStruct((BLK, H * DH)...  38.4 us
    unnamed x2, local copies, waits for them, and re-layouts  2.65 us

profile of v4, /device:TPU:1, one launch (start us, length us, event | category | flops | bytes accessed | tf_op | source)
XLA Modules:
  0.0 42.3 jit_solution(15884720007996388021)
XLA Ops:
  1.3 38.4 %star.1 = (bf16[256,8192]{1,0:T(8,128)(2,1)S(1)}, f32[64,128]{1,0:T(8,128)S(1)}) custom-call(bf16[256,8192]{1,0:T(8,128)(2,1)} %q_hbm.1, bf16[256,1024]{1,0:T(8,128)(2,1)} %k_hbm.1, bf16[256,1024]{1,0:T(8,128)(2,1)} %v_hbm.1, bf16[1,8192]{1,0:T(2,128)(2,1)} %question_hbm.1, s32[128]{0:T(128)} %valid_hbm.1, s32[1]{0:T(128)S(6)} %copy.12.qlen_ref), custom_call_target="tpu_custom_call" | custom-call | tf_op jit(solution)/shard_map/star/pallas_call | solution.py:429
  39.7 0.6 %copy.10 = bf16[1,1,64,128]{3,1,2,0:T(2,128)(2,1)} copy(bf16[1,1,64,128]{3,2,1,0:T(8,128)(2,1)S(1)} %convert_bitcast_fusion) | data formatting | bytes 32768
  40.3 2.0 %copy.13 = bf16[256,8192]{1,0:T(8,128)(2,1)} copy(bf16[256,8192]{1,0:T(8,128)(2,1)S(1)} %get-tuple-element.8) | data formatting | bytes 8388608
  (1 shorter events, 0.0 us)

commit v5 on v4

--- a/solution.py
+++ b/solution.py
@@ -22,8 +22,8 @@
 ORDER = (0, 1, 3, 2)
 NT = (((1,), (1,)), ((), ()))
 
-ROWS_AT = 2
-SPREAD_AT = 2
+ROWS_AT = 1
+SPREAD_AT = 1
 GATHER_AT = 2
 MERGE_AT = 2
 GREETINGS = 9 + 1 + 15 + 7 + 7
@@ -239,13 +239,13 @@
             lax.fori_loop(1, 16, send_q, 0)
 
 
-        @pl.when(n == 2)
+        @pl.when(n == 1)
         def _():
             @pl.when(me <= 1)
             def _():
                 lax.fori_loop(1, 8, send_kv, 0)
 
-        for g in (2 * n, 2 * n + 1):
+        for g in (4 * n, 4 * n + 1, 4 * n + 2, 4 * n + 3):
             base = pl.multiple_of(g * 512, 512)
             keys = kvs[pl.ds(base, 256), :]
             values = jnp.concatenate([kvs[pl.ds(base + 256, 256), :], ones_own], axis=1)
@@ -260,7 +260,7 @@
                 own_lse[:, cols] = jnp.where(live, peak + jnp.log2(o[:, DH:]), DEAD)
         return carry
 
-    lax.fori_loop(0, KVH // 2, own_block, 0)
+    lax.fori_loop(0, KVH // 4, own_block, 0)
 
     gather()
 

time: 42.4 us -> 42.4 us (level)
  no operation moved by 1% of the time
where the time goes in v5:
time: 42.4 us; the launch traced here: 42.2 us
  Pallas kernels  38.3 us (90%)
  local copies, waits for them, and re-layouts  2.65 us (6%)
  between operations  1.29 us (3%)
    pallas_call x1, Pallas kernels, body(): pl.pallas_call(star_kernel, out_shape=(jax.ShapeDtypeStruct((BLK, H * DH)...  38.3 us
    unnamed x2, local copies, waits for them, and re-layouts  2.65 us

profile of v5, /device:TPU:1, one launch (start us, length us, event | category | flops | bytes accessed | tf_op | source)
XLA Modules:
  0.0 42.2 jit_solution(15048663532665936408)
XLA Ops:
  1.3 38.3 %star.1 = (bf16[256,8192]{1,0:T(8,128)(2,1)S(1)}, f32[64,128]{1,0:T(8,128)S(1)}) custom-call(bf16[256,8192]{1,0:T(8,128)(2,1)} %q_hbm.1, bf16[256,1024]{1,0:T(8,128)(2,1)} %k_hbm.1, bf16[256,1024]{1,0:T(8,128)(2,1)} %v_hbm.1, bf16[1,8192]{1,0:T(2,128)(2,1)} %question_hbm.1, s32[128]{0:T(128)} %valid_hbm.1, s32[1]{0:T(128)S(6)} %copy.12.qlen_ref), custom_call_target="tpu_custom_call" | custom-call | tf_op jit(solution)/shard_map/star/pallas_call | solution.py:429
  39.6 0.6 %copy.10 = bf16[1,1,64,128]{3,1,2,0:T(2,128)(2,1)} copy(bf16[1,1,64,128]{3,2,1,0:T(8,128)(2,1)S(1)} %convert_bitcast_fusion) | data formatting | bytes 32768
  40.2 2.0 %copy.13 = bf16[256,8192]{1,0:T(8,128)(2,1)} copy(bf16[256,8192]{1,0:T(8,128)(2,1)S(1)} %get-tuple-element.8) | data formatting | bytes 8388608
  (1 shorter events, 0.0 us)
